TPU v7x, 256 devices: a whole 4x4x8 slice. The times are simulated.
256 devices in a mesh: band: 32 (over z, x), gvec: 8 (over y, core).
Axes of the slice: x: 4, y: 4, z: 8, core: 2. Of those that a mesh axis runs over, the one named last changes fastest.
Arguments:
- pairs: bfloat16 [32, 8, 512, 640], P(None, 'gvec', 'band'), may hold values from -0.59765625 to 0.59765625
- cond_energy: float32 [512], replicated, may hold values from 0.5 to 12
- val_energy: float32 [32, 8], replicated, may hold values from -12 to -2
- band_counts: int32 [32], replicated, may hold values from 1 to 16, as said below
- slab: int32 [1], replicated, may hold values from 0 to 31
Outputs:
- chi_zero: float32 [20480, 20480], P('gvec', 'band')
Inputs may be any that keep to these rules, and one draw needn't show every extreme that they name: `band_counts`: every owner has at least one occupied slot, and in every draw some owner has all 16 slots occupied.
All inputs are finite; a program needn't handle non-finite values.
Results may differ from a plain program's by a relative error of at most 0.0028.
Values may be sent and summed in bfloat16 or wider, within the bound.
No kernel may reach another device: no remote copies, remote signals or barrier semaphores. Data moves between devices by JAX's collectives and lax.ppermute only.
A program may use at most 128 MiB of HBM per device.

v0:
```python
import jax
import jax.numpy as jnp
from jax import lax
from jax.sharding import PartitionSpec as P


def on_device(pairs, cond_energy, val_energy, band_counts, slab):
    n_band = lax.axis_size("band")
    n_gvec = lax.axis_size("gvec")
    ratio = n_band // n_gvec
    local_v = pairs.shape[1]
    slot_count = pairs.shape[2]
    col_width = pairs.shape[3]
    energies = lax.dynamic_index_in_dim(val_energy, slab[0], 0, keepdims=False)
    slots = jnp.arange(slot_count, dtype=jnp.int32)
    live = (slots[None, :] < band_counts[:, None]).reshape(-1)
    weight = jnp.where(
        live[None, :], 2.0 / (energies[:, None] - cond_energy[None, :]), jnp.float32(0.0)
    )
    blocked = pairs.reshape(n_gvec, ratio, local_v, slot_count, col_width)
    by_block = lax.all_to_all(blocked, "gvec", split_axis=0, concat_axis=2, tiled=True)
    rows_all = lax.all_gather(by_block, "band", axis=3, tiled=True)[0]
    by_column = lax.all_to_all(pairs, "band", split_axis=0, concat_axis=2, tiled=True)
    cols_all = lax.all_gather(by_column, "gvec", axis=1, tiled=True)[0]
    scaled = (weight[:, :, None] * cols_all.astype(jnp.float32)).astype(jnp.bfloat16)
    result = lax.dot_general(
        rows_all, scaled, (((1, 2), (0, 1)), ((), ())), preferred_element_type=jnp.float32
    )
    return result.reshape(ratio * col_width, col_width)


def solution(mesh):
    in_specs = (P(None, "gvec", "band", None), P(), P(), P(), P())
    out_specs = P("gvec", "band")
    return jax.shard_map(
        on_device, mesh=mesh, in_specs=in_specs, out_specs=out_specs, check_vma=False
    )
```

profile of v0, /device:TPU:1, one launch (start us, length us, event | category | flops | bytes accessed | tf_op | source)
XLA Modules:
  0.0 263.4 jit_solution(6837848196494836438)
XLA Ops:
  6.5 0.0 copy-start
  6.5 0.0 all-gather.6.cloned.1.call-start
  6.5 17.7 %all_to_all.30 = bf16[8,4,1,16,640]{4,3,2,1,0:T(8,128)(2,1)S(1)} all-to-all(bf16[8,4,1,16,640]{4,3,2,1,0:T(8,128)(2,1)} %bitcast.24), channel_id=1, replica_groups=mesh['band'=32,'gvec'=8] {'gvec'}, dimensions={0} | all-to-all | bytes 1310720 | tf_op jit(solution)/shard_map/all_to_all | solution.py:21
  24.3 1.2 copy.8
  25.5 0.0 all-gather.6.cloned.1.call-update
  25.5 0.0 all-gather.4.cloned.1.call-start
  25.6 32.6 %all_to_all.31 = bf16[32,1,16,640]{3,2,1,0:T(8,128)(2,1)} all-to-all(bf16[32,1,16,640]{3,2,1,0:T(8,128)(2,1)} %param.5), channel_id=1, replica_groups=mesh['band'=32,'gvec'=8] {'band'}, dimensions={0} | all-to-all | bytes 1310720 | tf_op jit(solution)/shard_map/all_to_all | solution.py:23
  58.2 0.0 all-gather.4.cloned.1.call-update
  58.8 0.7 iota_compare_fusion
  59.6 0.1 lt.27
  59.7 0.0 copy-done
  59.7 0.2 dynamic-slice_reduce_fusion
  59.8 0.8 divide_select_fusion
  60.6 133.8 %all-gather.6.cloned.1.call-done = bf16[1,4,8,1,512,640]{5,2,3,1,0,4:T(8,128)(2,1)} async-done(((bf16[1,4,8,1,16,640]{5,2,3,1,0,4:T(8,128)(2,1)}), bf16[1,4,8,1,512,640]{5,2,3,1,0,4:T(8,128)(2,1)}) %all-gather.6.cloned.1.call-update) | async-done | bytes 20971536 | tf_op jit(solution)/shard_map/all_gather | solution.py:22
  194.4 30.2 %copy.9 = bf16[1,4,8,1,512,640]{4,5,2,1,3,0:T(8,128)(2,1)} copy(bf16[1,4,8,1,512,640]{5,2,3,1,0,4:T(8,128)(2,1)} %all-gather.6.cloned.1.call-done) | data formatting | bytes 41943040 | tf_op jit(solution)/shard_map/all_gather | solution.py:22
  224.6 8.6 %all-gather.4.cloned.1.call-done = bf16[1,8,512,640]{3,2,0,1:T(8,128)(2,1)} async-done(((bf16[1,1,512,640]{3,2,0,1:T(8,128)(2,1)}), bf16[1,8,512,640]{3,2,0,1:T(8,128)(2,1)}) %all-gather.4.cloned.1.call-update) | async-done | bytes 5242896 | tf_op jit(solution)/shard_map/all_gather | solution.py:24
  233.3 23.3 %fusion = f32[640,4,640,1]{0,2,3,1:T(8,128)} fusion(bf16[1,4,8,1,512,640]{4,5,2,1,3,0:T(8,128)(2,1)} %copy.9, bf16[1,8,512,640]{3,2,0,1:T(8,128)(2,1)} %all-gather.4.cloned.1.call-done, f32[8,512]{1,0:T(8,128)S(1)} %divide_select_fusion), kind=kOutput, calls=%fused_computation | convolution fusion | flops 13429637120 | bytes 32784384 | tf_op jit(solution)/shard_map/dot_general | solution.py:26
Async XLA Ops:
  6.5 53.1 %copy-start = (f32[32,8]{0,1:T(8,128)S(1)}, f32[32,8]{0,1:T(8,128)}, u32[]{:S(2)}) copy-start(f32[32,8]{0,1:T(8,128)} %param.7) | copy-start | bytes 3076
  6.5 187.9 %all-gather.6.cloned.1.call-start = ((), (), s32[]{:S(2)}) async-start(), calls=%async_computation.3 | async-start | bytes 21626880 | tf_op jit(solution)/shard_map/all_gather | solution.py:22
  25.5 207.7 %all-gather.4.cloned.1.call-start = ((), (), s32[]{:S(2)}) async-start(), calls=%async_computation.2 | async-start | bytes 5898240 | tf_op jit(solution)/shard_map/all_gather | solution.py:24
Sparse Core Ops, SparseCore 0:
  25.6 168.7 all-gather.5
  196.3 36.9 all-gather.3
where the time goes:
time: 264 us; the launch traced here: 263 us
  waiting for transfers between devices  142 us (54%)
  blocking collectives  50.3 us (19%)
  local copies, waits for them, and re-layouts  31.7 us (12%)
  matrix products  23.3 us (9%)
  between operations  14.1 us (5%)
    all_gather x1, waiting for transfers between devices, on_device(): rows_all = lax.all_gather(by_block, 'band', axis=3, tiled=True)[0]  134 us
    all_to_all x1, blocking collectives, on_device(): lax.all_to_all(pairs, 'band', split_axis=0, concat_axis=2, tiled=True)  32.6 us
    all_gather x1, local copies, waits for them, and re-layouts, on_device(): rows_all = lax.all_gather(by_block, 'band', axis=3, tiled=True)[0]  30.2 us
    dot_general x1, matrix products, on_device(): lax.dot_general(rows_all, scaled, (((1, 2), (0, 1)), ((), ())), preferred...  23.3 us
    all_to_all x1, blocking collectives, on_device(): lax.all_to_all(blocked, 'gvec', split_axis=0, concat_axis=2, tiled=True)  17.7 us
    all_gather x1, waiting for transfers between devices, on_device(): cols_all = lax.all_gather(by_column, 'gvec', axis=1, tiled=True)[0]  8.62 us
  transfers between devices with their start and end apart: 2, of which 2 were waited for; matrix products, arithmetic and copies ran while one was open for 12% of the time, Pallas kernels for 0%

commit v1 on v0

--- a/solution.py
+++ b/solution.py
@@ -2,6 +2,15 @@
 import jax.numpy as jnp
 from jax import lax
 from jax.sharding import PartitionSpec as P
+
+
+def define_cycles_here(arr_in):
+    return jnp.concatenate(
+        lax.all_to_all(
+            jnp.stack(tuple((arr_in for _ in range(lax.psum(1, "gvec"))))), "gvec", 0, 0
+        ),
+        axis=1,
+    )
 
 
 def on_device(pairs, cond_energy, val_energy, band_counts, slab):
@@ -21,7 +30,7 @@
     by_block = lax.all_to_all(blocked, "gvec", split_axis=0, concat_axis=2, tiled=True)
     rows_all = lax.all_gather(by_block, "band", axis=3, tiled=True)[0]
     by_column = lax.all_to_all(pairs, "band", split_axis=0, concat_axis=2, tiled=True)
-    cols_all = lax.all_gather(by_column, "gvec", axis=1, tiled=True)[0]
+    cols_all = define_cycles_here(by_column)[0]
     scaled = (weight[:, :, None] * cols_all.astype(jnp.float32)).astype(jnp.bfloat16)
     result = lax.dot_general(
         rows_all, scaled, (((1, 2), (0, 1)), ((), ())), preferred_element_type=jnp.float32

time: 264 us -> 256 us (0.970)
  waiting for transfers between devices: 142 us -> 124 us
  starting transfers between devices: 0.04 us -> 8.68 us
    all_gather x1, waiting for transfers between devices: 134 us -> 124 us  [on_device(): rows_all = lax.all_gather(by_block, 'band', axis=3, tiled=True)[0]]
    all_to_all x0 -> x1, starting transfers between devices: none -> 8.68 us  [define_cycles_here(): lax.all_to_all(jnp.stack(tuple((arr_in for _ in range(lax.psum(1, 'gvec')...]
    all_gather x1 -> x0, waiting for transfers between devices: 8.62 us -> none  [on_device(): cols_all = lax.all_gather(by_column, 'gvec', axis=1, tiled=True)[0]]
    another operation x0 -> x1, local copies, waits for them, and re-layouts: none -> 2.78 us  [define_cycles_here(): jnp.stack(tuple((arr_in for _ in range(lax.psum(1, 'gvec')))))]
  transfers between devices with their start and end apart: 2 -> 2, of which waited for: 2 -> 1; matrix products, arithmetic and copies ran while one was open for 12% -> 13% of each run, Pallas kernels for 0% -> 0%
where the time goes in v1:
time: 256 us; the launch traced here: 255 us
  waiting for transfers between devices  124 us (48%)
  blocking collectives  50.3 us (20%)
  local copies, waits for them, and re-layouts  34.3 us (13%)
  matrix products  23.3 us (9%)
  between operations  14.1 us (6%)
  starting transfers between devices  8.68 us (3%)
    all_gather x1, waiting for transfers between devices, on_device(): rows_all = lax.all_gather(by_block, 'band', axis=3, tiled=True)[0]  124 us
    all_to_all x1, blocking collectives, on_device(): lax.all_to_all(pairs, 'band', split_axis=0, concat_axis=2, tiled=True)  32.5 us
    all_gather x1, local copies, waits for them, and re-layouts, on_device(): rows_all = lax.all_gather(by_block, 'band', axis=3, tiled=True)[0]  30.1 us
    dot_general x1, matrix products, on_device(): lax.dot_general(rows_all, scaled, (((1, 2), (0, 1)), ((), ())), preferred...  23.3 us
    all_to_all x1, blocking collectives, on_device(): lax.all_to_all(blocked, 'gvec', split_axis=0, concat_axis=2, tiled=True)  17.8 us
    all_to_all x1, starting transfers between devices, define_cycles_here(): lax.all_to_all(jnp.stack(tuple((arr_in for _ in range(lax.psum(1, 'gvec')...  8.68 us
  transfers between devices with their start and end apart: 2, of which 1 were waited for; matrix products, arithmetic and copies ran while one was open for 13% of the time, Pallas kernels for 0%

profile of v1, /device:TPU:1, one launch (start us, length us, event | category | flops | bytes accessed | tf_op | source)
XLA Modules:
  0.0 254.7 jit_solution(16022949856824807583)
XLA Ops:
  6.5 0.0 copy-start
  6.5 0.0 all-gather.3.cloned.1.call-start
  6.5 0.0 copy-start.2
  6.5 0.0 copy-start.1
  6.5 17.8 %all_to_all.32 = bf16[8,4,1,16,640]{4,3,2,1,0:T(8,128)(2,1)S(1)} all-to-all(bf16[8,4,1,16,640]{4,3,2,1,0:T(8,128)(2,1)} %bitcast.25), channel_id=1, replica_groups=mesh['band'=32,'gvec'=8] {'gvec'}, dimensions={0} | all-to-all | bytes 1310720 | tf_op jit(solution)/shard_map/all_to_all | solution.py:30
  24.3 1.2 copy.8
  25.5 0.0 all-gather.3.cloned.1.call-update
  25.5 32.5 %all_to_all.33 = bf16[32,1,16,640]{3,2,1,0:T(8,128)(2,1)S(1)} all-to-all(bf16[32,1,16,640]{3,2,1,0:T(8,128)(2,1)} %param.5), channel_id=1, replica_groups=mesh['band'=32,'gvec'=8] {'band'}, dimensions={0} | all-to-all | bytes 1310720 | tf_op jit(solution)/shard_map/all_to_all | solution.py:32
  58.1 2.8 %stack.5 = bf16[8,1,1,512,640]{4,3,2,1,0:T(8,128)(2,1)} broadcast(bf16[512,640]{1,0:T(8,128)(2,1)S(1)} %bitcast.27), dimensions={3,4} | broadcast | bytes 5898240 | tf_op jit(solution)/shard_map/stack | solution.py:10
  60.9 8.7 %all-to-all-start.1 = ((bf16[8,1,1,512,640]{4,3,2,1,0:T(8,128)(2,1)}), bf16[8,1,1,512,640]{4,3,2,1,0:T(8,128)(2,1)}, u32[]{:S(2)}, u32[]{:S(2)}) async-start(bf16[8,1,1,512,640]{4,3,2,1,0:T(8,128)(2,1)} %stack.5), calls=%async_computation.1 | async-start | bytes 10485760 | tf_op jit(solution)/shard_map/all_to_all | solution.py:9
  70.2 0.0 copy-done.2
  70.2 0.1 iota_compare_fusion
  70.3 0.1 lt.27
  70.4 0.0 copy-done
  70.4 0.2 dynamic-slice_reduce_fusion
  70.6 0.0 copy-done.1
  70.6 0.1 divide_select_fusion
  70.6 123.8 %all-gather.3.cloned.1.call-done = bf16[1,4,8,1,512,640]{5,2,3,1,0,4:T(8,128)(2,1)} async-done(((bf16[1,4,8,1,16,640]{5,2,3,1,0,4:T(8,128)(2,1)}), bf16[1,4,8,1,512,640]{5,2,3,1,0,4:T(8,128)(2,1)}) %all-gather.3.cloned.1.call-update) | async-done | bytes 20971536 | tf_op jit(solution)/shard_map/all_gather | solution.py:31
  194.5 30.1 %copy.9 = bf16[1,4,8,1,512,640]{4,5,2,1,3,0:T(8,128)(2,1)} copy(bf16[1,4,8,1,512,640]{5,2,3,1,0,4:T(8,128)(2,1)} %all-gather.3.cloned.1.call-done) | data formatting | bytes 41943040 | tf_op jit(solution)/shard_map/all_gather | solution.py:31
  224.5 0.0 all-to-all-done.1
  224.5 23.3 %fusion = f32[640,4,640,1]{0,2,3,1:T(8,128)} fusion(bf16[1,4,8,1,512,640]{4,5,2,1,3,0:T(8,128)(2,1)} %copy.9, bf16[8,1,1,512,640]{4,3,2,1,0:T(8,128)(2,1)} %all-to-all-done.1, f32[8,512]{1,0:T(8,128)S(1)} %divide_select_fusion), kind=kOutput, calls=%fused_computation | convolution fusion | flops 13429637120 | bytes 32784384 | tf_op jit(solution)/shard_map/dot_general | solution.py:35
Async XLA Ops:
  6.5 63.8 %copy-start = (f32[32,8]{0,1:T(8,128)S(1)}, f32[32,8]{0,1:T(8,128)}, u32[]{:S(2)}) copy-start(f32[32,8]{0,1:T(8,128)} %param.7) | copy-start | bytes 3076
  6.5 187.9 %all-gather.3.cloned.1.call-start = ((), (), s32[]{:S(2)}) async-start(), calls=%async_computation.3 | async-start | bytes 21626880 | tf_op jit(solution)/shard_map/all_gather | solution.py:31
  6.5 63.7 %copy-start.2 = (s32[32]{0:T(128)S(1)}, s32[32]{0:T(128)}, u32[]{:S(2)}) copy-start(s32[32]{0:T(128)} %param.8) | copy-start | bytes 388
  6.5 64.0 %copy-start.1 = (f32[512]{0:T(512)S(1)}, f32[512]{0:T(512)}, u32[]{:S(2)}) copy-start(f32[512]{0:T(512)} %param.6) | copy-start | bytes 6148
  60.9 163.7 %all-to-all-start.1 = ((bf16[8,1,1,512,640]{4,3,2,1,0:T(8,128)(2,1)}), bf16[8,1,1,512,640]{4,3,2,1,0:T(8,128)(2,1)}, u32[]{:S(2)}, u32[]{:S(2)}) async-start(bf16[8,1,1,512,640]{4,3,2,1,0:T(8,128)(2,1)} %stack.5), calls=%async_computation.1 | async-start | bytes 10485760 | tf_op jit(solution)/shard_map/all_to_all | solution.py:9
Sparse Core Ops, SparseCore 0:
  25.7 168.7 all-gather.2
